TPU v7x, 32 devices: a whole 2x2x4 slice. The times are simulated.
32 devices in a mesh: dp: 4 (over y, x), head: 8 (over z, core).
Axes of the slice: x: 2, y: 2, z: 4, core: 2. Of those that a mesh axis runs over, the one named last changes fastest.
Arguments:
- query_latent: bfloat16 [1024, 1536], P('dp'), may hold values from -384 to 384
- kv_latent: bfloat16 [1024, 576], P('dp'), may hold values from -48 to 48
- out_grad: bfloat16 [1024, 4096], P('dp', 'head'), may hold values from -20 to 20
- query_up: bfloat16 [1536, 6144], P(None, 'head'), may hold values from -1 to 1
- key_up: bfloat16 [512, 4096], P(None, 'head'), may hold values from -0.25 to 0.25
- value_up: bfloat16 [512, 4096], P(None, 'head'), may hold values from -0.25 to 0.25
Outputs:
- query_latent_grad: float32 [1024, 1536], P(('dp', 'head'))
- kv_latent_grad: float32 [1024, 576], P(('dp', 'head'))
- query_up_grad: bfloat16 [1536, 6144], P(None, 'head')
- key_up_grad: bfloat16 [512, 4096], P(None, 'head')
- value_up_grad: bfloat16 [512, 4096], P(None, 'head')
All inputs are finite; a program needn't handle non-finite values.
Results may differ from a plain program's by a relative error of at most 0.035.
Values may be sent and summed in bfloat16 or wider, within the bound.
No kernel may reach another device: no remote copies, remote signals or barrier semaphores. Data moves between devices by JAX's collectives and lax.ppermute only.
A program may use at most 64 MiB of HBM per device.

v0:
```python
import functools

import jax
import jax.numpy as jnp
import numpy as np
from jax import lax
from jax.experimental import pallas as pl
from jax.experimental.pallas import tpu as pltpu
from jax.sharding import PartitionSpec as P

QL = 1536
KL = 512
DN = 128
DR = 64
TILE = 128
WIDTH = DN + DR
PAIR = 2 * WIDTH
LATENT = QL + KL + DR

max_rms = 1.0
eps = 1e-06
VMEM_LIMIT = 32 * 2**20

NT = (((1,), (1,)), ((), ()))
TN = (((0,), (0,)), ((), ()))


def dot(left, right, dims=(((1,), (0,)), ((), ()))):
    return lax.dot_general(left, right, dims, preferred_element_type=jnp.float32)


def rotary_tables(length):
    half = DR // 2
    freqs = np.float32(10000.0) ** (
        np.float32(-2.0) * np.arange(half, dtype=np.float32) / np.float32(DR)
    )
    angle = np.arange(length, dtype=np.float32)[:, None] * freqs.astype(np.float32)[None, :]
    cosine, sine = np.cos(angle), np.sin(angle)
    ones, zeros = np.ones((length, DR), np.float32), np.zeros((length, DR), np.float32)
    return np.concatenate([cosine, cosine, ones, -sine, sine, zeros], axis=1)


def swap_halves(tile):
    lane = lax.broadcasted_iota(jnp.int32, tile.shape, 1)
    first = lane % DR < DR // 2
    return jnp.where(
        first, pltpu.roll(tile, TILE - DR // 2, 1), pltpu.roll(tile, DR // 2, 1)
    )


def rounded(values):
    return values.astype(jnp.bfloat16).astype(jnp.float32)


def softmax_grads(scores, grad_probs):
    length = scores.shape[0]
    block = length // 2
    scale = 1.0 / (DN + DR) ** 0.5
    key = lax.broadcasted_iota(jnp.int32, (block, block), 0)
    query = lax.broadcasted_iota(jnp.int32, (block, block), 1)
    allowed = key <= query
    grad_probs = rounded(grad_probs)
    probs_columns, grads_columns = [], []
    for column in range(2):
        columns = slice(column * block, (column + 1) * block)
        parts = [scores[:block, columns], scores[block:, columns]][: column + 1]
        parts[-1] = jnp.where(allowed, parts[-1], -jnp.inf)
        tops = [jnp.max(part, axis=0, keepdims=True) for part in parts]
        top = tops[0] if column == 0 else jnp.maximum(*tops)
        parts = [jnp.exp((part - top) * scale) for part in parts]
        sums = [jnp.sum(part, axis=0, keepdims=True) for part in parts]
        inverse = 1.0 / (sums[0] if column == 0 else sums[0] + sums[1])
        parts = [part * inverse for part in parts]
        grads = [grad_probs[:block, columns], grad_probs[block:, columns]][: column + 1]
        means = [jnp.sum(g * p, axis=0, keepdims=True) for g, p in zip(grads, parts)]
        mean = means[0] if column == 0 else means[0] + means[1]
        grads = [(p * (g - mean) * scale).astype(jnp.bfloat16) for g, p in zip(grads, parts)]
        parts = [p.astype(jnp.bfloat16) for p in parts]
        if column == 0:
            parts.append(jnp.zeros((block, block), jnp.bfloat16))
            grads.append(jnp.zeros((block, block), jnp.bfloat16))
        probs_columns.append(jnp.concatenate(parts, axis=0))
        grads_columns.append(jnp.concatenate(grads, axis=0))
    return jnp.concatenate(probs_columns, axis=1), jnp.concatenate(grads_columns, axis=1)


def backward(length, xq, xkv, grad, weights, table, gq, gkv, qw, kw, vw, rot_out, ready):
    wq, wk, wv = weights
    n_seq = xq.shape[0] // length
    wide = wk.shape[1]
    heads = wide // DN
    low = lax.broadcasted_iota(jnp.int32, (length, TILE), 1) < DR
    spans = [slice(s * length, (s + 1) * length) for s in range(n_seq)]

    ready[0]()
    cos_low, sin_low = table[:, :TILE], table[:, TILE:]
    cos_tiles = (cos_low, pltpu.roll(cos_low, DR, 1))
    sin_tiles = (sin_low, pltpu.roll(sin_low, DR, 1))
    latent = xkv[:, :KL]
    for pair in range(heads // 2):
        columns = slice(2 * DN * pair, 2 * DN * (pair + 1))
        keys = dot(latent, wk[:, columns])
        vw[:, columns] = dot(latent, wv[:, columns]).astype(jnp.bfloat16)
        for span in spans:
            rot = jnp.concatenate(
                [xkv[span, KL : KL + DR].astype(jnp.float32), jnp.zeros((length, DR), jnp.float32)],
                axis=1,
            )
            odd = pltpu.roll(keys[span, DN:], DR, 1)
            tiles = (
                keys[span, :DN],
                rot,
                jnp.where(low, 0.0, odd),
                jnp.where(low, odd, pltpu.roll(rot, DR, 1)),
            )
            for i, tile in enumerate(tiles):
                start = (4 * pair + i) * TILE
                kw[span, start : start + TILE] = tile.astype(jnp.bfloat16)
    ready[1]()
    for pair in range(heads // 2):
        queries = dot(xq[...], wq[:, PAIR * pair : PAIR * (pair + 1)])
        for span in spans:
            for i in range(3):
                part = rounded(queries[span, i * TILE : (i + 1) * TILE])
                if i > 0:
                    part = part * cos_tiles[i - 1] + swap_halves(part) * sin_tiles[i - 1]
                start = PAIR * pair + i * TILE
                qw[span, start : start + TILE] = part.astype(jnp.bfloat16)

    items = [(span, head) for span in spans for head in range(heads)]

    def windows(span, head):
        start = PAIR * (head // 2) + TILE * (head % 2)
        return (
            qw[span, start : start + 2 * TILE],
            kw[span, 2 * TILE * head : 2 * TILE * (head + 1)],
            slice(head * DN, (head + 1) * DN),
        )

    def first_products(span, head):
        query_window, key_window, columns = windows(span, head)
        return (
            dot(key_window, query_window, NT),
            dot(vw[span, columns], grad[span, columns], NT),
        )

    rot_sums = [jnp.zeros((length, TILE), jnp.float32) for _ in spans]
    pending = first_products(*items[0])
    even_part = None
    for index, (span, head) in enumerate(items):
        products = pending
        if index + 1 < len(items):
            pending = first_products(*items[index + 1])
        probs, grad_scores = softmax_grads(*products)
        query_window, key_window, columns = windows(span, head)
        gkv[span, wide + head * DN : wide + (head + 1) * DN] = dot(probs, grad[span, columns]).astype(
            jnp.bfloat16
        )
        key_part = dot(grad_scores, query_window)
        query_part = dot(grad_scores, key_window, TN)
        seq = index // heads
        if head % 2 == 0:
            gkv[span, columns] = key_part[:, :TILE].astype(jnp.bfloat16)
            if rot_out is not None:
                rot_sums[seq] = rot_sums[seq] + rounded(key_part[:, TILE:])
            even_part = query_part
            continue
        turned = pltpu.roll(key_part[:, TILE:], DR, 1)
        gkv[span, columns] = jnp.where(low, pltpu.roll(key_part[:, :TILE], DR, 1), turned).astype(
            jnp.bfloat16
        )
        if rot_out is not None:
            rot_sums[seq] = rot_sums[seq] + rounded(turned)
        parts = [
            even_part[:, :TILE],
            even_part[:, TILE:] + query_part[:, :TILE],
            query_part[:, TILE:],
        ]
        for i in range(3):
            part = parts[i]
            if i > 0:
                part = rounded(part)
                part = part * cos_tiles[i - 1] - swap_halves(part) * sin_tiles[i - 1]
            start = PAIR * (head // 2) + i * TILE
            gq[span, start : start + TILE] = part.astype(jnp.bfloat16)
    if rot_out is not None:
        rot_out[...] = rot_sums[0]


def raw_grads(xq, xkv, gq, gkv, previous, emit):
    wide = gkv.shape[1] // 2
    step = KL
    for block in range(QL // step + 1):
        if block < QL // step:
            rows = slice(block * step, (block + 1) * step)
            targets = ((0, rows, dot(xq[:, rows], gq[...], TN)),)
        else:
            rows = slice(0, KL)
            product = dot(xkv[:, :KL], gkv[...], TN)
            targets = ((1, rows, product[:, :wide]), (2, rows, product[:, wide:]))
        for which, rows, product in targets:
            if previous is not None:
                product = product + previous[which][rows, :]
            emit(which, rows, product)


def load_kernel(place, xq, kvt, grad, packed, kv_rows, sem):
    half, wide = packed.shape[0], grad.shape[1]
    width = QL + KL + TILE
    rows = pl.ds(pl.multiple_of(place[1] * half, half), half)
    pieces = (
        (kvt.at[:, rows], kv_rows),
        (xq.at[rows], packed.at[:, :QL]),
        (grad.at[:half], packed.at[:, width : width + wide]),
        (grad.at[half:], packed.at[:, width + wide :]),
    )
    copies = [pltpu.make_async_copy(*piece, sem.at[i]) for i, piece in enumerate(pieces)]
    for copy in copies:
        copy.start()
    copies[0].wait()
    for block in range(0, KL + DR, TILE):
        stop = min(block + TILE, KL + DR)
        packed[:, QL + block : QL + stop] = kv_rows[block:stop, :].T
    packed[:, LATENT:width] = jnp.zeros((half, TILE - DR), jnp.bfloat16)
    for copy in copies[1:]:
        copy.wait()


def own_kernel(n_head, place, xq_in, kvt_in, grad_in, wq_in, wk_in, wv_in, table_in, *refs):
    wq, wk, wv, table, xq, xkv, gq, gkv, keep, send_stay, send_go, *refs = refs
    kvt, grad, qw, kw, vw, term, sem = refs
    pieces = (
        (kvt_in, kvt),
        (table_in, table),
        (wk_in, wk),
        (wv_in, wv),
        (xq_in, xq),
        (wq_in, wq),
        (grad_in, grad),
    )
    copies = [pltpu.make_async_copy(*piece, sem.at[i]) for i, piece in enumerate(pieces)]
    for copy in copies:
        copy.start()

    def latents_ready():
        for copy in copies[:4]:
            copy.wait()
        for block in range(0, KL + DR, TILE):
            stop = min(block + TILE, KL + DR)
            xkv[:, block:stop] = kvt[block:stop, :].T

    def queries_ready():
        for copy in copies[4:]:
            copy.wait()

    length = xq.shape[0]
    rot = term.at[:, QL + KL :]
    ready = (latents_ready, queries_ready)
    backward(length, xq, xkv, grad, (wq, wk, wv), table, gq, gkv, qw, kw, vw, rot, ready)
    wide = wk.shape[1]
    term[:, :QL] = dot(gq[...], wq[...], NT)
    term[:, QL : QL + KL] = dot(gkv[:, :wide], wk[...], NT) + dot(gkv[:, wide:], wv[...], NT)
    rows = length // n_head
    chip, core = place[0], place[1]
    masks = [turned_round(k, n_head // 2) for k in range(n_head // 2)]

    def chosen(which):
        starts = [(2 * jnp.bitwise_xor(chip, mask) + which) * rows for mask in masks]
        return jnp.concatenate([term[pl.ds(pl.multiple_of(i, rows), rows), :] for i in starts])

    keep[...] = chosen(core)
    send = chosen(1 - core).astype(jnp.bfloat16)
    send_stay[...] = send[: send_stay.shape[0], :]
    send_go[...] = send[send_stay.shape[0] :, :]


def fold_kernel(keep, *refs):
    received, (stay, go) = refs[:-2], refs[-2:]
    total = jnp.concatenate([part[...] for part in received]).astype(jnp.float32) + keep[...]
    stay[...] = total[: stay.shape[0], :]
    go[...] = total[stay.shape[0] :, :].astype(jnp.bfloat16)


def far_kernel(n_seq, place, *refs):
    blocks, refs = refs[: 2 * n_seq], refs[2 * n_seq :]
    wq, wk, wv, table, xq, xkv, gq, gkv, grad, qw, kw, vw = refs
    half, wide = blocks[0].shape[0], grad.shape[1]
    length = 2 * half
    width = QL + KL + TILE
    core = place[1]
    for s in range(n_seq):
        mine, other = blocks[2 * s : 2 * s + 2]
        for source, side in ((mine, core), (other, 1 - core)):
            rows = pl.ds(pl.multiple_of(s * length + side * half, half), half)
            xq[rows, :] = source[:, :QL]
            xkv[rows, :] = source[:, QL:LATENT]
        start = s * length
        grad[start : start + half, :] = mine[:, width : width + wide]
        grad[start + half : start + length, :] = mine[:, width + wide :]
    ready = (lambda: None, lambda: None)
    backward(length, xq, xkv, grad, (wq, wk, wv), table, gq, gkv, qw, kw, vw, None, ready)


def sums_kernel(first, with_squares, xq, xkv, gq, gkv, *refs):
    previous, refs = (None, refs) if first else (refs[:3], refs[3:])
    taken = None
    if with_squares and not first:
        taken, *refs = refs
    sums = refs[:3]
    totals = [jnp.zeros((8, TILE), jnp.float32)]

    def emit(which, rows, block):
        sums[which][rows, :] = block
        if not with_squares:
            return
        folded = jnp.zeros((8, block.shape[1]), jnp.float32)
        for start in range(rows.start, rows.stop, 64):
            part = sums[which][start : start + 64, :]
            folded = folded + jnp.sum((part * part).reshape(8, 8, part.shape[1]), axis=0)
        for column in range(0, block.shape[1], TILE):
            totals[0] = totals[0] + folded[:, column : column + TILE]

    raw_grads(xq, xkv, gq, gkv, previous, emit)
    if with_squares:
        refs[3][...] = totals[0] if first else totals[0] - taken[...]


def add_kernel(*refs):
    total = refs[0][...]
    for ref in refs[1:-1]:
        total = total + ref[...]
    refs[-1][...] = total


def final_kernel(limit, n_parts, share, xq, xkv, gq, gkv, *refs):
    previous, (local, received), refs = refs[:3], refs[3:5], refs[5:]
    parts, refs = refs[:n_parts], refs[n_parts:]
    outs, (latent_q, latent_kv), buffers, sem = refs[:3], refs[3:5], refs[5:8], refs[8]
    total = parts[0][...]
    for part in parts[1:]:
        total = total + part[...]
    total = jnp.maximum(jnp.sum(total, keepdims=True) * share, 0.0)
    factor = jnp.minimum(1.0, limit / jnp.sqrt(total + eps))
    copies = []

    def emit(which, rows, block):
        buffers[which][rows, :] = (block * factor).astype(jnp.bfloat16)
        copy = pltpu.make_async_copy(
            buffers[which].at[rows], outs[which].at[rows], sem.at[len(copies)]
        )
        copy.start()
        copies.append(copy)

    raw_grads(xq, xkv, gq, gkv, previous, emit)
    terms = local[...] + received[...].astype(jnp.float32)
    latent_q[...] = terms[:, :QL]
    latent_kv[...] = terms[:, QL:LATENT]
    for copy in copies:
        copy.wait()


def vmem(count):
    return [pl.BlockSpec(memory_space=pltpu.VMEM)] * count


def hbm(count):
    return [pl.BlockSpec(memory_space=pltpu.HBM)] * count


def params():
    return pltpu.CompilerParams(vmem_limit_bytes=VMEM_LIMIT)


def free():
    return pl.CostEstimate(flops=0, bytes_accessed=0, transcendentals=0)


def struct(shape, dtype):
    return jax.ShapeDtypeStruct(shape, dtype)


def exchange(value, axis, size, k):
    return lax.ppermute(value, axis, [(i, i ^ k) for i in range(size)])


def far_away(value):
    return pltpu.with_memory_space_constraint(value, pltpu.HBM)


def turned_round(mask, n_dp):
    bits = n_dp.bit_length() - 1
    return sum(((mask >> i) & 1) << (bits - 1 - i) for i in range(bits))


def across(value, n_dp, n_head, mask):
    masks = (mask, turned_round(mask, n_dp))
    pairs = [
        (d * n_head + h, (d ^ masks[h % 2]) * n_head + h) for d in range(n_dp) for h in range(n_head)
    ]
    return lax.ppermute(value, ("dp", "head"), pairs)


def per_device(n_dp, n_head, query_latent, kv_latent, out_grad, query_up, key_up, value_up):
    length = query_latent.shape[0]
    half = length // 2
    wide_q, wide_k = query_up.shape[1], key_up.shape[1]
    heads = wide_k // DN
    index = lax.axis_index("head")
    place = jnp.stack([index // 2, index % 2]).astype(jnp.int32)
    table = jnp.asarray(rotary_tables(length))
    smem = [pl.BlockSpec(memory_space=pltpu.SMEM)]
    inputs = [far_away(value) for value in (query_latent, kv_latent.T, out_grad)]
    width = QL + KL + TILE

    packed = pl.pallas_call(
        load_kernel,
        out_shape=pltpu.VMEM((half, width + 2 * wide_k), jnp.bfloat16),
        in_specs=smem + hbm(3),
        out_specs=pl.BlockSpec(memory_space=pltpu.VMEM),
        scratch_shapes=[pltpu.VMEM((KL + DR, half), jnp.bfloat16), pltpu.SemaphoreType.DMA((4,))],
        compiler_params=params(),
        cost_estimate=free(),
        name="load",
    )(place, *inputs)
    packed, place = lax.optimization_barrier((packed, place))
    singles = [1 << i for i in reversed(range(n_dp.bit_length() - 1))]
    received = {k: across(packed, n_dp, n_head, k) for k in singles}

    def rows_shape(rows):
        widths = (QL, KL + DR, wide_q, 2 * wide_k)
        return tuple(pltpu.VMEM((rows, width), jnp.bfloat16) for width in widths)

    def scratch(rows):
        widths = (wide_k, wide_q, 2 * TILE * heads, wide_k)
        return [pltpu.VMEM((rows, width), jnp.bfloat16) for width in widths]

    weights_shape = tuple(
        pltpu.VMEM(shape, jnp.bfloat16) for shape in ((QL, wide_q), (KL, wide_k), (KL, wide_k))
    )
    sums_shape = tuple(pltpu.VMEM(w.shape, jnp.float32) for w in weights_shape)
    *outs, keep, send_stay, send_go = pl.pallas_call(
        functools.partial(own_kernel, n_head),
        out_shape=(
            *weights_shape,
            pltpu.VMEM(table.shape, jnp.float32),
            *rows_shape(length),
            struct((half, width), jnp.float32),
            struct((half // 2, width), jnp.bfloat16),
            struct((half // 2, width), jnp.bfloat16),
        ),
        in_specs=smem + hbm(7),
        out_specs=vmem(11),
        scratch_shapes=[pltpu.VMEM((KL + DR, length), jnp.bfloat16)]
        + scratch(length)
        + [pltpu.VMEM((length, width), jnp.float32), pltpu.SemaphoreType.DMA((7,))],
        compiler_params=params(),
        cost_estimate=free(),
        name="own",
    )(place, *inputs, *[far_away(value) for value in (query_up, key_up, value_up, table)])
    weights, found = outs[:4], outs[4:]

    rows, n_chip = length // n_head, n_head // 2
    squares_shape = struct((8, TILE), jnp.float32)

    def add_sums(found, sums, with_squares, taken=()):
        extra_out = (squares_shape,) if with_squares else ()
        return list(
            pl.pallas_call(
                functools.partial(sums_kernel, not sums, with_squares),
                out_shape=(*sums_shape, *extra_out),
                in_specs=vmem(4 + len(sums) + len(taken)),
                out_specs=vmem(3 + len(extra_out)),
                input_output_aliases={4: 0, 5: 1, 6: 2} if sums else {},
                compiler_params=params(),
                cost_estimate=free(),
                name="sums",
            )(*found, *sums, *taken)
        )

    def add(*values):
        return pl.pallas_call(
            add_kernel,
            out_shape=squares_shape,
            in_specs=vmem(len(values)),
            out_specs=pl.BlockSpec(memory_space=pltpu.VMEM),
            compiler_params=params(),
            cost_estimate=free(),
            name="add",
        )(*values)

    *sums, own_squares = add_sums(found, [], True)

    def fold(keep, *received):
        half_shape = (keep.shape[0] // 2, width)
        return pl.pallas_call(
            fold_kernel,
            out_shape=(struct(half_shape, jnp.float32), struct(half_shape, jnp.bfloat16)),
            in_specs=vmem(1 + len(received)),
            out_specs=vmem(2),
            compiler_params=params(),
            cost_estimate=free(),
            name="fold",
        )(keep, *received)

    stay, go = fold(keep, *[exchange(send, "head", n_head, 1) for send in (send_stay, send_go)])
    bits = [2 << i for i in range(n_head.bit_length() - 2)]
    for bit in bits[:-2]:
        stay, go = fold(stay, exchange(go, "head", n_head, bit))
    came = exchange(go, "head", n_head, bits[-2])

    values = [received[k] for k in singles]
    *values, sums[2], came = lax.optimization_barrier((*values, sums[2], came))
    received = dict(zip(singles, values))
    for k in range(3, n_dp):
        if k not in received:
            received[k] = across(received[k & (k - 1)], n_dp, n_head, k & -k)
    stay, go = fold(stay, came)
    terms = [stay, exchange(go, "head", n_head, bits[-1])]

    def swapped(k):
        return exchange(received[turned_round(k, n_dp)], "head", n_head, 1)

    groups = [(1, 2)] + [(k,) for k in range(3, n_dp)]
    for index, group in enumerate(groups):
        n_seq = len(group)
        blocks = []
        for k in group:
            blocks += [received[k], swapped(k)]
        last = index == len(groups) - 1
        if last:
            blocks[1], *parts = lax.optimization_barrier((blocks[1], *parts))
            squares = add(*parts)
            parts = [squares] + [exchange(squares, "dp", n_dp, k) for k in range(1, n_dp)]
        found = list(
            pl.pallas_call(
                functools.partial(far_kernel, n_seq),
                out_shape=rows_shape(n_seq * length),
                in_specs=smem + vmem(len(blocks) + 4),
                out_specs=vmem(4),
                scratch_shapes=scratch(n_seq * length),
                compiler_params=params(),
                cost_estimate=free(),
                name="far",
            )(place, *blocks, *weights)
        )
        if last:
            break
        if index == 0:
            found[3], terms[1] = lax.optimization_barrier((found[3], terms[1]))
        if index < len(groups) - 2:
            sums = add_sums(found, sums, False)
        else:
            *sums, squares = add_sums(found, sums, True, [own_squares])
            squares = add(squares, exchange(squares, "head", n_head, 1))
            parts = [squares] + [exchange(squares, "head", n_head, 2 * k) for k in range(1, n_chip)]
        k = groups[index + 1][0]
        received[k], sums[2] = lax.optimization_barrier((received[k], sums[2]))

    count = (QL * wide_q + 2 * KL * wide_k) * n_head
    limit = max_rms * count**0.5
    *scaled, latent_q, latent_kv = pl.pallas_call(
        functools.partial(final_kernel, limit, len(parts), 1.0 / (n_dp - 2)),
        out_shape=(
            *[struct(w.shape, jnp.bfloat16) for w in weights_shape],
            struct((rows, QL), jnp.float32),
            struct((rows, KL + DR), jnp.float32),
        ),
        in_specs=vmem(4 + 3 + 2 + len(parts)),
        out_specs=hbm(3) + vmem(2),
        scratch_shapes=list(weights_shape) + [pltpu.SemaphoreType.DMA((QL // KL + 2,))],
        compiler_params=params(),
        cost_estimate=free(),
        name="final",
    )(*found, *sums, *terms, *parts)
    return (latent_q, latent_kv, *scaled)


def solution(mesh):
    placed = (
        P("dp", None),
        P("dp", None),
        P("dp", "head"),
        P(None, "head"),
        P(None, "head"),
        P(None, "head"),
    )
    return jax.shard_map(
        functools.partial(per_device, mesh.shape["dp"], mesh.shape["head"]),
        mesh=mesh,
        in_specs=placed,
        out_specs=(
            P(("dp", "head"), None),
            P(("dp", "head"), None),
            P(None, "head"),
            P(None, "head"),
            P(None, "head"),
        ),
        check_vma=False,
    )
```

profile of v0, /device:TPU:0, one launch (start us, length us, event | category | flops | bytes accessed | tf_op | source)
XLA Modules:
  0.0 59.5 jit_solution(7003792767612797449)
XLA Ops:
  0.7 1.7 %load.1 = bf16[128,3200]{1,0:T(8,128)(2,1)S(1)} custom-call(s32[2]{0:T(128)S(1)} %pad_add_fusion.place, bf16[256,1536]{1,0:T(8,128)(2,1)} %xq_in.1, bf16[576,256]{1,0:T(8,128)(2,1)} %bitcast.3, bf16[256,512]{1,0:T(8,128)(2,1)} %grad_in.1), custom_call_target="tpu_custom_call" | custom-call | tf_op jit(solution)/shard_map/load/pallas_call | solution.py:415
  2.5 3.0 %collective-permute-start.1 = (bf16[128,3200]{1,0:T(8,128)(2,1)S(1)}, bf16[128,3200]{1,0:T(8,128)(2,1)S(1)}, u32[]{:S(2)}, u32[]{:S(2)}) collective-permute-start(bf16[128,3200]{1,0:T(8,128)(2,1)S(1)} %load.1), channel_id=1, source_target_pairs={{0,8},{1,17},{2,10},{3,19},{4,12},{5,21},{6,14},{7,23},{8,0},{9,25... | collective-permute-start | bytes 2457608 | tf_op jit(solution)/shard_map/ppermute | solution.py:400
  5.5 1.5 %collective-permute-start = (bf16[128,3200]{1,0:T(8,128)(2,1)S(1)}, bf16[128,3200]{1,0:T(8,128)(2,1)S(1)}, u32[]{:S(2)}, u32[]{:S(2)}) collective-permute-start(bf16[128,3200]{1,0:T(8,128)(2,1)S(1)} %load.1), channel_id=1, source_target_pairs={{0,16},{1,9},{2,18},{3,11},{4,20},{5,13},{6,22},{7,15},{8,24},{9,1... | collective-permute-start | bytes 2457608 | tf_op jit(solution)/shard_map/ppermute | solution.py:400
  7.0 6.1 %own.1 = (bf16[1536,768]{1,0:T(8,128)(2,1)S(1)}, bf16[512,512]{1,0:T(8,128)(2,1)S(1)}, bf16[512,512]{1,0:T(8,128)(2,1)S(1)}, f32[256,256]{1,0:T(8,128)S(1)}, bf1...) custom-call(s32[2]{0:T(128)S(1)} %pad_add_fusion.place, ...), custom_call_target="tpu_custom_call" | custom-call | tf_op jit(solution)/shard_map/own/pallas_call | solution.py:441
  13.2 0.5 collective-permute-start.3
  13.7 1.0 %collective-permute-done.2.refs_0_ = bf16[64,2176]{1,0:T(8,128)(2,1)S(1)} collective-permute-done((bf16[64,2176]{1,0:T(8,128)(2,1)S(1)}, bf16[64,2176]{1,0:T(8,128)(2,1)S(1)}, u32[]{:S(2)}, u32[]{:S(2)}) %collective-permute-start.2) | collective-permute-done | bytes 278560 | tf_op jit(solution)/shard_map/ppermute | solution.py:383
  15.3 1.6 %collective-permute-start.4 = (bf16[64,2176]{1,0:T(8,128)(2,1)S(1)}, bf16[64,2176]{1,0:T(8,128)(2,1)S(1)}, u32[]{:S(2)}, u32[]{:S(2)}) collective-permute-start(bf16[64,2176]{1,0:T(8,128)(2,1)S(1)} %get-tuple-element.66), channel_id=1, source_target_pairs={{0,2},{1,3},{2,0},{3,1},{4,6},{5,7},{6,4},{7,5},{8,10},{9,11},{10,... | collective-permute-start | bytes 835592 | tf_op jit(solution)/shard_map/ppermute | solution.py:383
  16.9 1.1 %sums.2 = (f32[1536,768]{1,0:T(8,128)S(1)}, f32[512,512]{1,0:T(8,128)S(1)}, f32[512,512]{1,0:T(8,128)S(1)}, f32[8,128]{1,0:T(8,128)S(1)}) custom-call(bf16[256,1536]{1,0:T(8,128)(2,1)S(1)} %get-tuple-element.58.xq, bf16[256,576]{1,0:T(8,128)(2,1)S(1)} %get-tuple-element.59.xkv, bf16[256,768]{1,0:T(8,128)(2,1)S(1)} %get-tuple-element.60.gq, ...), custom_call_target="tpu_custom_call" | custom-call | tf_op jit(solution)/shard_map/sums/pallas_call | solution.py:468
  18.0 6.0 %collective-permute-done.4.refs_0_ = bf16[64,2176]{1,0:T(8,128)(2,1)S(1)} collective-permute-done((bf16[64,2176]{1,0:T(8,128)(2,1)S(1)}, bf16[64,2176]{1,0:T(8,128)(2,1)S(1)}, u32[]{:S(2)}, u32[]{:S(2)}) %collective-permute-start.4) | collective-permute-done | bytes 278560 | tf_op jit(solution)/shard_map/ppermute | solution.py:383
  24.6 2.4 %collective-permute-start.5 = (bf16[128,3200]{1,0:T(8,128)(2,1)S(1)}, bf16[128,3200]{1,0:T(8,128)(2,1)S(1)}, u32[]{:S(2)}, u32[]{:S(2)}) collective-permute-start(bf16[128,3200]{1,0:T(8,128)(2,1)S(1)} %collective-permute-done.refs_2_), channel_id=1, source_target_pairs={{0,8},{1,17},{2,10},{3,19},{4,12},{5,21},{6,14},{7,23},{8,0},{9,25... | collective-permute-start | bytes 2457608 | tf_op jit(solution)/shard_map/ppermute | solution.py:400
  27.0 2.7 %collective-permute-start.8 = (bf16[32,2176]{1,0:T(8,128)(2,1)S(1)}, bf16[32,2176]{1,0:T(8,128)(2,1)S(1)}, u32[]{:S(2)}, u32[]{:S(2)}) collective-permute-start(bf16[32,2176]{1,0:T(8,128)(2,1)S(1)} %get-tuple-element.79), channel_id=1, source_target_pairs={{0,4},{1,5},{2,6},{3,7},{4,0},{5,1},{6,2},{7,3},{8,12},{9,13},{10,... | collective-permute-start | bytes 417800 | tf_op jit(solution)/shard_map/ppermute | solution.py:383
  29.7 5.3 %far.2 = (bf16[512,1536]{1,0:T(8,128)(2,1)S(1)}, bf16[512,576]{1,0:T(8,128)(2,1)S(1)}, bf16[512,768]{1,0:T(8,128)(2,1)S(1)}, bf16[512,1024]{1,0:T(8,128)(2,1)S(1)}) custom-call(s32[2]{0:T(128)S(1)} %pad_add_fusion.place, bf16[128,3200]{1,0:T(8,128)(2,1)S(1)} %collective-permute-done.1.refs_0_, bf16[128,3200]{1,0:T(8,128)(2,1)S(1)} %collective-permute-done.6.refs_1_, ...), custom_call_target="tpu_custom_call" | custom-call | tf_op jit(solution)/shard_map/far/pallas_call | solution.py:535
  35.5 3.4 %sums.3 = (f32[1536,768]{1,0:T(8,128)S(1)}, f32[512,512]{1,0:T(8,128)S(1)}, f32[512,512]{1,0:T(8,128)S(1)}, f32[8,128]{1,0:T(8,128)S(1)}) custom-call(bf16[512,1536]{1,0:T(8,128)(2,1)S(1)} %get-tuple-element.73.xq, bf16[512,576]{1,0:T(8,128)(2,1)S(1)} %get-tuple-element.74.xkv, ...), custom_call_target="tpu_custom_call", output_to_operand_aliasing={{0}: (4, {}), {1}: (5, {}), {2}: (6, {})} | custom-call | tf_op jit(solution)/shard_map/sums/pallas_call | solution.py:468
  38.9 0.5 collective-permute-start.10
  39.4 1.8 %collective-permute-done.10.refs_1_ = f32[8,128]{1,0:T(8,128)S(1)} collective-permute-done((f32[8,128]{1,0:T(8,128)S(1)}, f32[8,128]{1,0:T(8,128)S(1)}, u32[]{:S(2)}, u32[]{:S(2)}) %collective-permute-start.10) | collective-permute-done | bytes 4128 | tf_op jit(solution)/shard_map/ppermute | solution.py:383
  41.3 3.5 %collective-permute-start.13 = (f32[8,128]{1,0:T(8,128)S(1)}, f32[8,128]{1,0:T(8,128)S(1)}, u32[]{:S(2)}, u32[]{:S(2)}) collective-permute-start(f32[8,128]{1,0:T(8,128)S(1)} %add.10.refs_0_), channel_id=1, source_target_pairs={{0,6},{1,7},{2,4},{3,5},{4,2},{5,3},{6,0},{7,1},{8,14},{9,15},{10,... | collective-permute-start | bytes 12296 | tf_op jit(solution)/shard_map/ppermute | solution.py:383
  44.8 0.8 %collective-permute-start.11 = (f32[8,128]{1,0:T(8,128)S(1)}, f32[8,128]{1,0:T(8,128)S(1)}, u32[]{:S(2)}, u32[]{:S(2)}) collective-permute-start(f32[8,128]{1,0:T(8,128)S(1)} %add.10.refs_0_), channel_id=1, source_target_pairs={{0,2},{1,3},{2,0},{3,1},{4,6},{5,7},{6,4},{7,5},{8,10},{9,11},{10,... | collective-permute-start | bytes 12296 | tf_op jit(solution)/shard_map/ppermute | solution.py:383
  45.7 1.0 %collective-permute-done.13.refs_3_ = f32[8,128]{1,0:T(8,128)S(1)} collective-permute-done((f32[8,128]{1,0:T(8,128)S(1)}, f32[8,128]{1,0:T(8,128)S(1)}, u32[]{:S(2)}, u32[]{:S(2)}) %collective-permute-start.13) | collective-permute-done | bytes 4128 | tf_op jit(solution)/shard_map/ppermute | solution.py:383
  46.7 2.6 %collective-permute-done.12.refs_2_ = f32[8,128]{1,0:T(8,128)S(1)} collective-permute-done((f32[8,128]{1,0:T(8,128)S(1)}, f32[8,128]{1,0:T(8,128)S(1)}, u32[]{:S(2)}, u32[]{:S(2)}) %collective-permute-start.12) | collective-permute-done | bytes 4128 | tf_op jit(solution)/shard_map/ppermute | solution.py:383
  49.3 2.4 %collective-permute-start.16 = (f32[8,128]{1,0:T(8,128)S(1)}, f32[8,128]{1,0:T(8,128)S(1)}, u32[]{:S(2)}, u32[]{:S(2)}) collective-permute-start(f32[8,128]{1,0:T(8,128)S(1)} %add.11.refs_5_), channel_id=1, source_target_pairs={{0,24},{8,16},{16,8},{24,0},{1,25},{9,17},{17,9},{25,1},{2,26},{10... | collective-permute-start | bytes 12296 | tf_op jit(solution)/shard_map/ppermute | solution.py:383
  51.7 0.6 %collective-permute-start.15 = (f32[8,128]{1,0:T(8,128)S(1)}, f32[8,128]{1,0:T(8,128)S(1)}, u32[]{:S(2)}, u32[]{:S(2)}) collective-permute-start(f32[8,128]{1,0:T(8,128)S(1)} %add.11.refs_5_), channel_id=1, source_target_pairs={{0,16},{8,24},{16,0},{24,8},{1,17},{9,25},{17,1},{25,9},{2,18},{10... | collective-permute-start | bytes 12296 | tf_op jit(solution)/shard_map/ppermute | solution.py:383
  52.3 0.5 collective-permute-start.14
  52.9 3.1 %far.3 = (bf16[256,1536]{1,0:T(8,128)(2,1)S(1)}, bf16[256,576]{1,0:T(8,128)(2,1)S(1)}, bf16[256,768]{1,0:T(8,128)(2,1)S(1)}, bf16[256,1024]{1,0:T(8,128)(2,1)S(1)}) custom-call(s32[2]{0:T(128)S(1)} %pad_add_fusion.place, bf16[128,3200]{1,0:T(8,128)(2,1)S(1)} %collective-permute-done.5.refs_0_, bf16[128,3200]{1,0:T(8,128)(2,1)S(1)} %collective-permute-done.9.refs_1_, ...), custom_call_target="tpu_custom_call" | custom-call | tf_op jit(solution)/shard_map/far/pallas_call | solution.py:535
  56.0 3.4 %final.1 = (bf16[1536,768]{1,0:T(8,128)(2,1)}, bf16[512,512]{1,0:T(8,128)(2,1)}, bf16[512,512]{1,0:T(8,128)(2,1)}, f32[32,1536]{1,0:T(8,128)}, f32[32,576]{1,0:T(8,128)}) custom-call(bf16[256,1536]{1,0:T(8,128)(2,1)S(1)} %get-tuple-element.89.xq, bf16[256,576]{1,0:T(8,128)(2,1)S(1)} %get-tuple-element.90.xkv, bf16[256,768]{1,0:T(8,128)(2,1)S(1)} %get-tuple-element.91.gq, ...), custom_call_target="tpu_custom_call" | custom-call | tf_op jit(solution)/shard_map/final/pallas_call | solution.py:561
  (22 shorter events, 1.8 us)
Async XLA Ops:
  2.5 21.6 %collective-permute-start.1 = (bf16[128,3200]{1,0:T(8,128)(2,1)S(1)}, bf16[128,3200]{1,0:T(8,128)(2,1)S(1)}, u32[]{:S(2)}, u32[]{:S(2)}) collective-permute-start(bf16[128,3200]{1,0:T(8,128)(2,1)S(1)} %load.1), channel_id=1, source_target_pairs={{0,8},{1,17},{2,10},{3,19},{4,12},{5,21},{6,14},{7,23},{8,0},{9,25... | collective-permute-start | bytes 2457608 | tf_op jit(solution)/shard_map/ppermute | solution.py:400
  5.5 18.6 %collective-permute-start = (bf16[128,3200]{1,0:T(8,128)(2,1)S(1)}, bf16[128,3200]{1,0:T(8,128)(2,1)S(1)}, u32[]{:S(2)}, u32[]{:S(2)}) collective-permute-start(bf16[128,3200]{1,0:T(8,128)(2,1)S(1)} %load.1), channel_id=1, source_target_pairs={{0,16},{1,9},{2,18},{3,11},{4,20},{5,13},{6,22},{7,15},{8,24},{9,1... | collective-permute-start | bytes 2457608 | tf_op jit(solution)/shard_map/ppermute | solution.py:400
  13.1 1.6 %collective-permute-start.2 = (bf16[64,2176]{1,0:T(8,128)(2,1)S(1)}, bf16[64,2176]{1,0:T(8,128)(2,1)S(1)}, u32[]{:S(2)}, u32[]{:S(2)}) collective-permute-start(bf16[64,2176]{1,0:T(8,128)(2,1)S(1)} %get-tuple-element.64), channel_id=1, source_target_pairs={{0,1},{1,0},{2,3},{3,2},{4,5},{5,4},{6,7},{7,6},{8,9},{9,8},{10,11... | collective-permute-start | bytes 835592 | tf_op jit(solution)/shard_map/ppermute | solution.py:383
  13.2 1.9 %collective-permute-start.3 = (bf16[64,2176]{1,0:T(8,128)(2,1)S(1)}, bf16[64,2176]{1,0:T(8,128)(2,1)S(1)}, u32[]{:S(2)}, u32[]{:S(2)}) collective-permute-start(bf16[64,2176]{1,0:T(8,128)(2,1)S(1)} %get-tuple-element.65), channel_id=1, source_target_pairs={{0,1},{1,0},{2,3},{3,2},{4,5},{5,4},{6,7},{7,6},{8,9},{9,8},{10,11... | collective-permute-start | bytes 835592 | tf_op jit(solution)/shard_map/ppermute | solution.py:383
  15.3 8.8 %collective-permute-start.4 = (bf16[64,2176]{1,0:T(8,128)(2,1)S(1)}, bf16[64,2176]{1,0:T(8,128)(2,1)S(1)}, u32[]{:S(2)}, u32[]{:S(2)}) collective-permute-start(bf16[64,2176]{1,0:T(8,128)(2,1)S(1)} %get-tuple-element.66), channel_id=1, source_target_pairs={{0,2},{1,3},{2,0},{3,1},{4,6},{5,7},{6,4},{7,5},{8,10},{9,11},{10,... | collective-permute-start | bytes 835592 | tf_op jit(solution)/shard_map/ppermute | solution.py:383
  24.0 5.7 %collective-permute-start.7 = (bf16[128,3200]{1,0:T(8,128)(2,1)S(1)}, bf16[128,3200]{1,0:T(8,128)(2,1)S(1)}, u32[]{:S(2)}, u32[]{:S(2)}) collective-permute-start(bf16[128,3200]{1,0:T(8,128)(2,1)S(1)} %collective-permute-done.1.refs_0_), channel_id=1, source_target_pairs={{0,1},{1,0},{2,3},{3,2},{4,5},{5,4},{6,7},{7,6},{8,9},{9,8},{10,11... | collective-permute-start | bytes 2457608 | tf_op jit(solution)/shard_map/ppermute | solution.py:383
  24.4 5.3 %collective-permute-start.6 = (bf16[128,3200]{1,0:T(8,128)(2,1)S(1)}, bf16[128,3200]{1,0:T(8,128)(2,1)S(1)}, u32[]{:S(2)}, u32[]{:S(2)}) collective-permute-start(bf16[128,3200]{1,0:T(8,128)(2,1)S(1)} %collective-permute-done.refs_2_), channel_id=1, source_target_pairs={{0,1},{1,0},{2,3},{3,2},{4,5},{5,4},{6,7},{7,6},{8,9},{9,8},{10,11... | collective-permute-start | bytes 2457608 | tf_op jit(solution)/shard_map/ppermute | solution.py:383
  24.6 14.3 %collective-permute-start.5 = (bf16[128,3200]{1,0:T(8,128)(2,1)S(1)}, bf16[128,3200]{1,0:T(8,128)(2,1)S(1)}, u32[]{:S(2)}, u32[]{:S(2)}) collective-permute-start(bf16[128,3200]{1,0:T(8,128)(2,1)S(1)} %collective-permute-done.refs_2_), channel_id=1, source_target_pairs={{0,8},{1,17},{2,10},{3,19},{4,12},{5,21},{6,14},{7,23},{8,0},{9,25... | collective-permute-start | bytes 2457608 | tf_op jit(solution)/shard_map/ppermute | solution.py:400
  27.0 8.4 %collective-permute-start.8 = (bf16[32,2176]{1,0:T(8,128)(2,1)S(1)}, bf16[32,2176]{1,0:T(8,128)(2,1)S(1)}, u32[]{:S(2)}, u32[]{:S(2)}) collective-permute-start(bf16[32,2176]{1,0:T(8,128)(2,1)S(1)} %get-tuple-element.79), channel_id=1, source_target_pairs={{0,4},{1,5},{2,6},{3,7},{4,0},{5,1},{6,2},{7,3},{8,12},{9,13},{10,... | collective-permute-start | bytes 417800 | tf_op jit(solution)/shard_map/ppermute | solution.py:383
  38.9 10.5 %collective-permute-start.9 = (bf16[128,3200]{1,0:T(8,128)(2,1)S(1)}, bf16[128,3200]{1,0:T(8,128)(2,1)S(1)}, u32[]{:S(2)}, u32[]{:S(2)}) collective-permute-start(bf16[128,3200]{1,0:T(8,128)(2,1)S(1)} %collective-permute-done.5.refs_0_), channel_id=1, source_target_pairs={{0,1},{1,0},{2,3},{3,2},{4,5},{5,4},{6,7},{7,6},{8,9},{9,8},{10,11... | collective-permute-start | bytes 2457608 | tf_op jit(solution)/shard_map/ppermute | solution.py:383
  38.9 2.3 %collective-permute-start.10 = (f32[8,128]{1,0:T(8,128)S(1)}, f32[8,128]{1,0:T(8,128)S(1)}, u32[]{:S(2)}, u32[]{:S(2)}) collective-permute-start(f32[8,128]{1,0:T(8,128)S(1)} %get-tuple-element.87.refs_0_), channel_id=1, source_target_pairs={{0,1},{1,0},{2,3},{3,2},{4,5},{5,4},{6,7},{7,6},{8,9},{9,8},{10,11... | collective-permute-start | bytes 12296 | tf_op jit(solution)/shard_map/ppermute | solution.py:383
  41.3 5.4 %collective-permute-start.13 = (f32[8,128]{1,0:T(8,128)S(1)}, f32[8,128]{1,0:T(8,128)S(1)}, u32[]{:S(2)}, u32[]{:S(2)}) collective-permute-start(f32[8,128]{1,0:T(8,128)S(1)} %add.10.refs_0_), channel_id=1, source_target_pairs={{0,6},{1,7},{2,4},{3,5},{4,2},{5,3},{6,0},{7,1},{8,14},{9,15},{10,... | collective-permute-start | bytes 12296 | tf_op jit(solution)/shard_map/ppermute | solution.py:383
  44.8 4.5 %collective-permute-start.12 = (f32[8,128]{1,0:T(8,128)S(1)}, f32[8,128]{1,0:T(8,128)S(1)}, u32[]{:S(2)}, u32[]{:S(2)}) collective-permute-start(f32[8,128]{1,0:T(8,128)S(1)} %add.10.refs_0_), channel_id=1, source_target_pairs={{0,4},{1,5},{2,6},{3,7},{4,0},{5,1},{6,2},{7,3},{8,12},{9,13},{10,... | collective-permute-start | bytes 12296 | tf_op jit(solution)/shard_map/ppermute | solution.py:383
  44.8 4.5 %collective-permute-start.11 = (f32[8,128]{1,0:T(8,128)S(1)}, f32[8,128]{1,0:T(8,128)S(1)}, u32[]{:S(2)}, u32[]{:S(2)}) collective-permute-start(f32[8,128]{1,0:T(8,128)S(1)} %add.10.refs_0_), channel_id=1, source_target_pairs={{0,2},{1,3},{2,0},{3,1},{4,6},{5,7},{6,4},{7,5},{8,10},{9,11},{10,... | collective-permute-start | bytes 12296 | tf_op jit(solution)/shard_map/ppermute | solution.py:383
  49.3 6.6 %collective-permute-start.16 = (f32[8,128]{1,0:T(8,128)S(1)}, f32[8,128]{1,0:T(8,128)S(1)}, u32[]{:S(2)}, u32[]{:S(2)}) collective-permute-start(f32[8,128]{1,0:T(8,128)S(1)} %add.11.refs_5_), channel_id=1, source_target_pairs={{0,24},{8,16},{16,8},{24,0},{1,25},{9,17},{17,9},{25,1},{2,26},{10... | collective-permute-start | bytes 12296 | tf_op jit(solution)/shard_map/ppermute | solution.py:383
  51.7 4.2 %collective-permute-start.15 = (f32[8,128]{1,0:T(8,128)S(1)}, f32[8,128]{1,0:T(8,128)S(1)}, u32[]{:S(2)}, u32[]{:S(2)}) collective-permute-start(f32[8,128]{1,0:T(8,128)S(1)} %add.11.refs_5_), channel_id=1, source_target_pairs={{0,16},{8,24},{16,0},{24,8},{1,17},{9,25},{17,1},{25,9},{2,18},{10... | collective-permute-start | bytes 12296 | tf_op jit(solution)/shard_map/ppermute | solution.py:383
  52.3 3.6 %collective-permute-start.14 = (f32[8,128]{1,0:T(8,128)S(1)}, f32[8,128]{1,0:T(8,128)S(1)}, u32[]{:S(2)}, u32[]{:S(2)}) collective-permute-start(f32[8,128]{1,0:T(8,128)S(1)} %add.11.refs_5_), channel_id=1, source_target_pairs={{0,8},{8,0},{16,24},{24,16},{1,9},{9,1},{17,25},{25,17},{2,10},{10... | collective-permute-start | bytes 12296 | tf_op jit(solution)/shard_map/ppermute | solution.py:383
where the time goes:
time: 59.7 us; the launch traced here: 59.5 us
  Pallas kernels  24.3 us (41%)
  starting transfers between devices  20.8 us (35%)
  waiting for transfers between devices  13.4 us (22%)
  between operations  0.92 us (2%)
    ppermute x14, starting transfers between devices, exchange(): return lax.ppermute(value, axis, [(i, i ^ k) for i in range(size)])  13.9 us
    ppermute x14, waiting for transfers between devices, exchange(): return lax.ppermute(value, axis, [(i, i ^ k) for i in range(size)])  13.4 us
    pallas_call x2, Pallas kernels, per_device(): pl.pallas_call(functools.partial(far_kernel, n_seq), out_shape=rows_shape...  8.4 us
    ppermute x3, starting transfers between devices, across(): return lax.ppermute(value, ('dp', 'head'), pairs)  6.95 us
    pallas_call x1, Pallas kernels, per_device(): pl.pallas_call(functools.partial(own_kernel, n_head), out_shape=(*weights...  6.14 us
    pallas_call x2, Pallas kernels, add_sums(): pl.pallas_call(functools.partial(sums_kernel, not sums, with_squares), ou...  4.47 us
    pallas_call x1, Pallas kernels, per_device(): pl.pallas_call(functools.partial(final_kernel, limit, len(parts), 1.0 / (...  3.36 us
    pallas_call x1, Pallas kernels, per_device(): pl.pallas_call(load_kernel, out_shape=pltpu.VMEM((half, width + 2 * wide_...  1.72 us
  transfers between devices with their start and end apart: 17, of which 7 were waited for; matrix products, arithmetic and copies ran while one was open for 0% of the time, Pallas kernels for 32%

commit v1 on v0

--- a/solution.py
+++ b/solution.py
@@ -332,26 +332,28 @@
     refs[-1][...] = total
 
 
-def final_kernel(limit, n_parts, share, xq, xkv, gq, gkv, *refs):
-    previous, (local, received), refs = refs[:3], refs[3:5], refs[5:]
-    parts, refs = refs[:n_parts], refs[n_parts:]
-    outs, (latent_q, latent_kv), buffers, sem = refs[:3], refs[3:5], refs[5:8], refs[8]
-    total = parts[0][...]
-    for part in parts[1:]:
-        total = total + part[...]
-    total = jnp.maximum(jnp.sum(total, keepdims=True) * share, 0.0)
+def last_kernel(xq, xkv, gq, gkv, pq, pk, pv, sq, sk, sv):
+    sums = (sq, sk, sv)
+
+    def emit(which, rows, block):
+        sums[which][rows, :] = block
+
+    raw_grads(xq, xkv, gq, gkv, (pq, pk, pv), emit)
+
+
+def scale_kernel(limit, share, left, right, sq, sk, sv, local, received, *refs):
+    oq, ok, ov, latent_q, latent_kv, bq, bk, bv, sem = refs
+    total = jnp.sum(left[...] + right[...], keepdims=True)
+    total = jnp.maximum(total * share, 0.0)
     factor = jnp.minimum(1.0, limit / jnp.sqrt(total + eps))
     copies = []
-
-    def emit(which, rows, block):
-        buffers[which][rows, :] = (block * factor).astype(jnp.bfloat16)
-        copy = pltpu.make_async_copy(
-            buffers[which].at[rows], outs[which].at[rows], sem.at[len(copies)]
-        )
-        copy.start()
-        copies.append(copy)
-
-    raw_grads(xq, xkv, gq, gkv, previous, emit)
+    for source, buffer, out in ((sq, bq, oq), (sk, bk, ok), (sv, bv, ov)):
+        for start in range(0, source.shape[0], 256):
+            rows = slice(start, start + 256)
+            buffer[rows, :] = (source[rows, :] * factor).astype(jnp.bfloat16)
+            copy = pltpu.make_async_copy(buffer.at[rows], out.at[rows], sem.at[len(copies)])
+            copy.start()
+            copies.append(copy)
     terms = local[...] + received[...].astype(jnp.float32)
     latent_q[...] = terms[:, :QL]
     latent_kv[...] = terms[:, QL:LATENT]
@@ -514,11 +516,11 @@
     for k in range(3, n_dp):
         if k not in received:
             received[k] = across(received[k & (k - 1)], n_dp, n_head, k & -k)
-    stay, go = fold(stay, came)
-    terms = [stay, exchange(go, "head", n_head, bits[-1])]
-
     def swapped(k):
         return exchange(received[turned_round(k, n_dp)], "head", n_head, 1)
+
+    def hop(squares, axis, size, mask):
+        return add(squares, exchange(squares, axis, size, mask))
 
     groups = [(1, 2)] + [(k,) for k in range(3, n_dp)]
     for index, group in enumerate(groups):
@@ -528,9 +530,8 @@
             blocks += [received[k], swapped(k)]
         last = index == len(groups) - 1
         if last:
-            blocks[1], *parts = lax.optimization_barrier((blocks[1], *parts))
-            squares = add(*parts)
-            parts = [squares] + [exchange(squares, "dp", n_dp, k) for k in range(1, n_dp)]
+            blocks[1], squares = lax.optimization_barrier((blocks[1], squares))
+            came = exchange(squares, "head", n_head, bits[-1])
         found = list(
             pl.pallas_call(
                 functools.partial(far_kernel, n_seq),
@@ -546,32 +547,53 @@
         if last:
             break
         if index == 0:
-            found[3], terms[1] = lax.optimization_barrier((found[3], terms[1]))
+            came, found[3] = lax.optimization_barrier((came, found[3]))
+            stay, go = fold(stay, came)
+            terms = [stay, exchange(go, "head", n_head, bits[-1])]
         if index < len(groups) - 2:
             sums = add_sums(found, sums, False)
         else:
             *sums, squares = add_sums(found, sums, True, [own_squares])
-            squares = add(squares, exchange(squares, "head", n_head, 1))
-            parts = [squares] + [exchange(squares, "head", n_head, 2 * k) for k in range(1, n_chip)]
+            squares = hop(squares, "head", n_head, 1)
         k = groups[index + 1][0]
         received[k], sums[2] = lax.optimization_barrier((received[k], sums[2]))
+
+    came, found[3] = lax.optimization_barrier((came, found[3]))
+    squares = add(squares, came)
+    for bit in bits[1:-1]:
+        squares = hop(squares, "head", n_head, bit)
+    came = exchange(squares, "head", n_head, bits[0])
+    sums = pl.pallas_call(
+        last_kernel,
+        out_shape=sums_shape,
+        in_specs=vmem(4 + 3),
+        out_specs=vmem(3),
+        input_output_aliases={4: 0, 5: 1, 6: 2},
+        compiler_params=params(),
+        cost_estimate=free(),
+        name="last",
+    )(*found, *sums)
+    came, terms[1], *sums = lax.optimization_barrier((came, terms[1], *sums))
+    squares = add(squares, came)
+    for k in singles[:-1]:
+        squares = hop(squares, "dp", n_dp, k)
 
     count = (QL * wide_q + 2 * KL * wide_k) * n_head
     limit = max_rms * count**0.5
     *scaled, latent_q, latent_kv = pl.pallas_call(
-        functools.partial(final_kernel, limit, len(parts), 1.0 / (n_dp - 2)),
+        functools.partial(scale_kernel, limit, 1.0 / (n_dp - 2)),
         out_shape=(
             *[struct(w.shape, jnp.bfloat16) for w in weights_shape],
             struct((rows, QL), jnp.float32),
             struct((rows, KL + DR), jnp.float32),
         ),
-        in_specs=vmem(4 + 3 + 2 + len(parts)),
+        in_specs=vmem(7),
         out_specs=hbm(3) + vmem(2),
-        scratch_shapes=list(weights_shape) + [pltpu.SemaphoreType.DMA((QL // KL + 2,))],
+        scratch_shapes=list(weights_shape) + [pltpu.SemaphoreType.DMA(((QL + 2 * KL) // 256,))],
         compiler_params=params(),
         cost_estimate=free(),
-        name="final",
-    )(*found, *sums, *terms, *parts)
+        name="scale",
+    )(squares, exchange(squares, "dp", n_dp, singles[-1]), *sums, *terms)
     return (latent_q, latent_kv, *scaled)
 
 

time: 59.7 us -> 61.9 us (1.037)
  waiting for transfers between devices: 13.4 us -> 18.3 us
  starting transfers between devices: 20.8 us -> 17.1 us
  Pallas kernels: 24.3 us -> 25.4 us
    ppermute x14 -> x12, waiting for transfers between devices: 13.4 us -> 17.3 us  [exchange(): return lax.ppermute(value, axis, [(i, i ^ k) for i in range(size)])]
    ppermute x14 -> x12, starting transfers between devices: 13.9 us -> 10.2 us  [exchange(): return lax.ppermute(value, axis, [(i, i ^ k) for i in range(size)])]
    pallas_call x1 -> x2, Pallas kernels: 3.36 us -> 4.41 us  [the longest x1 2.73 us: per_device(): pl.pallas_call(functools.partial(scale_kernel, limit, 1.0 / (n_dp - 2)),...]
    ppermute x3, waiting for transfers between devices: 0.01 us -> 1.02 us  [across(): return lax.ppermute(value, ('dp', 'head'), pairs)]
  transfers between devices with their start and end apart: 17 -> 15, of which waited for: 7 -> 10; matrix products, arithmetic and copies ran while one was open for 0% -> 0% of each run, Pallas kernels for 32% -> 34%
where the time goes in v1:
time: 61.9 us; the launch traced here: 61.8 us
  Pallas kernels  25.4 us (41%)
  waiting for transfers between devices  18.3 us (30%)
  starting transfers between devices  17.1 us (28%)
  between operations  0.89 us (1%)
    ppermute x12, waiting for transfers between devices, exchange(): return lax.ppermute(value, axis, [(i, i ^ k) for i in range(size)])  17.3 us
    ppermute x12, starting transfers between devices, exchange(): return lax.ppermute(value, axis, [(i, i ^ k) for i in range(size)])  10.2 us
    pallas_call x2, Pallas kernels, per_device(): pl.pallas_call(functools.partial(far_kernel, n_seq), out_shape=rows_shape...  8.42 us
    ppermute x3, starting transfers between devices, across(): return lax.ppermute(value, ('dp', 'head'), pairs)  6.95 us
    pallas_call x1, Pallas kernels, per_device(): pl.pallas_call(functools.partial(own_kernel, n_head), out_shape=(*weights...  6.14 us
    pallas_call x2, Pallas kernels, add_sums(): pl.pallas_call(functools.partial(sums_kernel, not sums, with_squares), ou...  4.47 us
    pallas_call x1, Pallas kernels, per_device(): pl.pallas_call(functools.partial(scale_kernel, limit, 1.0 / (n_dp - 2)),...  2.73 us
    pallas_call x1, Pallas kernels, per_device(): pl.pallas_call(load_kernel, out_shape=pltpu.VMEM((half, width + 2 * wide_...  1.72 us
  transfers between devices with their start and end apart: 15, of which 10 were waited for; matrix products, arithmetic and copies ran while one was open for 0% of the time, Pallas kernels for 34%

profile of v1, /device:TPU:0, one launch (start us, length us, event | category | flops | bytes accessed | tf_op | source)
XLA Modules:
  0.0 61.8 jit_solution(5127183016523559655)
XLA Ops:
  0.7 1.7 %load.1 = bf16[128,3200]{1,0:T(8,128)(2,1)S(1)} custom-call(s32[2]{0:T(128)S(1)} %pad_add_fusion.place, bf16[256,1536]{1,0:T(8,128)(2,1)} %xq_in.1, bf16[576,256]{1,0:T(8,128)(2,1)} %bitcast.3, bf16[256,512]{1,0:T(8,128)(2,1)} %grad_in.1), custom_call_target="tpu_custom_call" | custom-call | tf_op jit(solution)/shard_map/load/pallas_call | solution.py:417
  2.5 3.0 %collective-permute-start.1 = (bf16[128,3200]{1,0:T(8,128)(2,1)S(1)}, bf16[128,3200]{1,0:T(8,128)(2,1)S(1)}, u32[]{:S(2)}, u32[]{:S(2)}) collective-permute-start(bf16[128,3200]{1,0:T(8,128)(2,1)S(1)} %load.1), channel_id=1, source_target_pairs={{0,8},{1,17},{2,10},{3,19},{4,12},{5,21},{6,14},{7,23},{8,0},{9,25... | collective-permute-start | bytes 2457608 | tf_op jit(solution)/shard_map/ppermute | solution.py:402
  5.5 1.5 %collective-permute-start = (bf16[128,3200]{1,0:T(8,128)(2,1)S(1)}, bf16[128,3200]{1,0:T(8,128)(2,1)S(1)}, u32[]{:S(2)}, u32[]{:S(2)}) collective-permute-start(bf16[128,3200]{1,0:T(8,128)(2,1)S(1)} %load.1), channel_id=1, source_target_pairs={{0,16},{1,9},{2,18},{3,11},{4,20},{5,13},{6,22},{7,15},{8,24},{9,1... | collective-permute-start | bytes 2457608 | tf_op jit(solution)/shard_map/ppermute | solution.py:402
  7.0 6.1 %own.1 = (bf16[1536,768]{1,0:T(8,128)(2,1)S(1)}, bf16[512,512]{1,0:T(8,128)(2,1)S(1)}, bf16[512,512]{1,0:T(8,128)(2,1)S(1)}, f32[256,256]{1,0:T(8,128)S(1)}, bf1...) custom-call(s32[2]{0:T(128)S(1)} %pad_add_fusion.place, ...), custom_call_target="tpu_custom_call" | custom-call | tf_op jit(solution)/shard_map/own/pallas_call | solution.py:443
  13.7 1.0 %collective-permute-done.2.refs_0_ = bf16[64,2176]{1,0:T(8,128)(2,1)S(1)} collective-permute-done((bf16[64,2176]{1,0:T(8,128)(2,1)S(1)}, bf16[64,2176]{1,0:T(8,128)(2,1)S(1)}, u32[]{:S(2)}, u32[]{:S(2)}) %collective-permute-start.2) | collective-permute-done | bytes 278560 | tf_op jit(solution)/shard_map/ppermute | solution.py:385
  15.3 1.6 %collective-permute-start.4 = (bf16[64,2176]{1,0:T(8,128)(2,1)S(1)}, bf16[64,2176]{1,0:T(8,128)(2,1)S(1)}, u32[]{:S(2)}, u32[]{:S(2)}) collective-permute-start(bf16[64,2176]{1,0:T(8,128)(2,1)S(1)} %get-tuple-element.73), channel_id=1, source_target_pairs={{0,2},{1,3},{2,0},{3,1},{4,6},{5,7},{6,4},{7,5},{8,10},{9,11},{10,... | collective-permute-start | bytes 835592 | tf_op jit(solution)/shard_map/ppermute | solution.py:385
  16.9 1.1 %sums.2 = (f32[1536,768]{1,0:T(8,128)S(1)}, f32[512,512]{1,0:T(8,128)S(1)}, f32[512,512]{1,0:T(8,128)S(1)}, f32[8,128]{1,0:T(8,128)S(1)}) custom-call(bf16[256,1536]{1,0:T(8,128)(2,1)S(1)} %get-tuple-element.65.xq, bf16[256,576]{1,0:T(8,128)(2,1)S(1)} %get-tuple-element.66.xkv, bf16[256,768]{1,0:T(8,128)(2,1)S(1)} %get-tuple-element.67.gq, ...), custom_call_target="tpu_custom_call" | custom-call | tf_op jit(solution)/shard_map/sums/pallas_call | solution.py:470
  18.0 6.0 %collective-permute-done.4.refs_0_ = bf16[64,2176]{1,0:T(8,128)(2,1)S(1)} collective-permute-done((bf16[64,2176]{1,0:T(8,128)(2,1)S(1)}, bf16[64,2176]{1,0:T(8,128)(2,1)S(1)}, u32[]{:S(2)}, u32[]{:S(2)}) %collective-permute-start.4) | collective-permute-done | bytes 278560 | tf_op jit(solution)/shard_map/ppermute | solution.py:385
  24.6 2.4 %collective-permute-start.5 = (bf16[128,3200]{1,0:T(8,128)(2,1)S(1)}, bf16[128,3200]{1,0:T(8,128)(2,1)S(1)}, u32[]{:S(2)}, u32[]{:S(2)}) collective-permute-start(bf16[128,3200]{1,0:T(8,128)(2,1)S(1)} %collective-permute-done.refs_2_), channel_id=1, source_target_pairs={{0,8},{1,17},{2,10},{3,19},{4,12},{5,21},{6,14},{7,23},{8,0},{9,25... | collective-permute-start | bytes 2457608 | tf_op jit(solution)/shard_map/ppermute | solution.py:402
  27.6 5.3 %far.2 = (bf16[512,1536]{1,0:T(8,128)(2,1)S(1)}, bf16[512,576]{1,0:T(8,128)(2,1)S(1)}, bf16[512,768]{1,0:T(8,128)(2,1)S(1)}, bf16[512,1024]{1,0:T(8,128)(2,1)S(1)}) custom-call(s32[2]{0:T(128)S(1)} %pad_add_fusion.place, bf16[128,3200]{1,0:T(8,128)(2,1)S(1)} %collective-permute-done.1.refs_0_, bf16[128,3200]{1,0:T(8,128)(2,1)S(1)} %collective-permute-done.6.refs_1_, ...), custom_call_target="tpu_custom_call" | custom-call | tf_op jit(solution)/shard_map/far/pallas_call | solution.py:536
  32.9 3.4 %sums.3 = (f32[1536,768]{1,0:T(8,128)S(1)}, f32[512,512]{1,0:T(8,128)S(1)}, f32[512,512]{1,0:T(8,128)S(1)}, f32[8,128]{1,0:T(8,128)S(1)}) custom-call(bf16[512,1536]{1,0:T(8,128)(2,1)S(1)} %get-tuple-element.80.xq, bf16[512,576]{1,0:T(8,128)(2,1)S(1)} %get-tuple-element.81.xkv, ...), custom_call_target="tpu_custom_call", output_to_operand_aliasing={{0}: (4, {}), {1}: (5, {}), {2}: (6, {})} | custom-call | tf_op jit(solution)/shard_map/sums/pallas_call | solution.py:470
  36.3 1.0 %collective-permute-done.5.refs_0_ = bf16[128,3200]{1,0:T(8,128)(2,1)S(1)} collective-permute-done((bf16[128,3200]{1,0:T(8,128)(2,1)S(1)}, bf16[128,3200]{1,0:T(8,128)(2,1)S(1)}, u32[]{:S(2)}, u32[]{:S(2)}) %collective-permute-start.5) | collective-permute-done | bytes 819232 | tf_op jit(solution)/shard_map/ppermute | solution.py:402
  37.4 3.2 %collective-permute-start.12 = (bf16[32,2176]{1,0:T(8,128)(2,1)S(1)}, bf16[32,2176]{1,0:T(8,128)(2,1)S(1)}, u32[]{:S(2)}, u32[]{:S(2)}) collective-permute-start(bf16[32,2176]{1,0:T(8,128)(2,1)S(1)} %get-tuple-element.99), channel_id=1, source_target_pairs={{0,4},{1,5},{2,6},{3,7},{4,0},{5,1},{6,2},{7,3},{8,12},{9,13},{10,... | collective-permute-start | bytes 417800 | tf_op jit(solution)/shard_map/ppermute | solution.py:385
  40.8 0.9 %collective-permute-done.9.refs_1_ = f32[8,128]{1,0:T(8,128)S(1)} collective-permute-done((f32[8,128]{1,0:T(8,128)S(1)}, f32[8,128]{1,0:T(8,128)S(1)}, u32[]{:S(2)}, u32[]{:S(2)}) %collective-permute-start.9) | collective-permute-done | bytes 4128 | tf_op jit(solution)/shard_map/ppermute | solution.py:385
  41.7 1.0 %collective-permute-start.10 = (f32[8,128]{1,0:T(8,128)S(1)}, f32[8,128]{1,0:T(8,128)S(1)}, u32[]{:S(2)}, u32[]{:S(2)}) collective-permute-start(f32[8,128]{1,0:T(8,128)S(1)} %add.12.refs_0_), channel_id=1, source_target_pairs={{0,4},{1,5},{2,6},{3,7},{4,0},{5,1},{6,2},{7,3},{8,12},{9,13},{10,... | collective-permute-start | bytes 12296 | tf_op jit(solution)/shard_map/ppermute | solution.py:385
  42.8 3.1 %far.3 = (bf16[256,1536]{1,0:T(8,128)(2,1)S(1)}, bf16[256,576]{1,0:T(8,128)(2,1)S(1)}, bf16[256,768]{1,0:T(8,128)(2,1)S(1)}, bf16[256,1024]{1,0:T(8,128)(2,1)S(1)}) custom-call(s32[2]{0:T(128)S(1)} %pad_add_fusion.place, bf16[128,3200]{1,0:T(8,128)(2,1)S(1)} %collective-permute-done.5.refs_0_, bf16[128,3200]{1,0:T(8,128)(2,1)S(1)} %collective-permute-done.8.refs_1_, ...), custom_call_target="tpu_custom_call" | custom-call | tf_op jit(solution)/shard_map/far/pallas_call | solution.py:536
  45.8 2.2 %collective-permute-done.10.refs_1_ = f32[8,128]{1,0:T(8,128)S(1)} collective-permute-done((f32[8,128]{1,0:T(8,128)S(1)}, f32[8,128]{1,0:T(8,128)S(1)}, u32[]{:S(2)}, u32[]{:S(2)}) %collective-permute-start.10) | collective-permute-done | bytes 4128 | tf_op jit(solution)/shard_map/ppermute | solution.py:385
  48.1 0.7 %collective-permute-start.11 = (f32[8,128]{1,0:T(8,128)S(1)}, f32[8,128]{1,0:T(8,128)S(1)}, u32[]{:S(2)}, u32[]{:S(2)}) collective-permute-start(f32[8,128]{1,0:T(8,128)S(1)} %add.13.refs_0_), channel_id=1, source_target_pairs={{0,2},{1,3},{2,0},{3,1},{4,6},{5,7},{6,4},{7,5},{8,10},{9,11},{10,... | collective-permute-start | bytes 12296 | tf_op jit(solution)/shard_map/ppermute | solution.py:385
  48.8 1.7 %last.1 = (f32[1536,768]{1,0:T(8,128)S(1)}, f32[512,512]{1,0:T(8,128)S(1)}, f32[512,512]{1,0:T(8,128)S(1)}) custom-call(bf16[256,1536]{1,0:T(8,128)(2,1)S(1)} %get-tuple-element.100.xq, bf16[256,576]{1,0:T(8,128)(2,1)S(1)} %get-tuple-element.101.xkv, ...), custom_call_target="tpu_custom_call", output_to_operand_aliasing={{0}: (4, {}), {1}: (5, {}), {2}: (6, {})} | custom-call | tf_op jit(solution)/shard_map/last/pallas_call | solution.py:566
  50.5 1.2 %collective-permute-done.11.refs_1_ = f32[8,128]{1,0:T(8,128)S(1)} collective-permute-done((f32[8,128]{1,0:T(8,128)S(1)}, f32[8,128]{1,0:T(8,128)S(1)}, u32[]{:S(2)}, u32[]{:S(2)}) %collective-permute-start.11) | collective-permute-done | bytes 4128 | tf_op jit(solution)/shard_map/ppermute | solution.py:385
  52.4 2.9 %collective-permute-done.13.refs_1_ = f32[8,128]{1,0:T(8,128)S(1)} collective-permute-done((f32[8,128]{1,0:T(8,128)S(1)}, f32[8,128]{1,0:T(8,128)S(1)}, u32[]{:S(2)}, u32[]{:S(2)}) %collective-permute-start.13) | collective-permute-done | bytes 4128 | tf_op jit(solution)/shard_map/ppermute | solution.py:385
  55.3 1.5 %collective-permute-start.14 = (f32[8,128]{1,0:T(8,128)S(1)}, f32[8,128]{1,0:T(8,128)S(1)}, u32[]{:S(2)}, u32[]{:S(2)}) collective-permute-start(f32[8,128]{1,0:T(8,128)S(1)} %add.15.left), channel_id=1, source_target_pairs={{0,8},{8,0},{16,24},{24,16},{1,9},{9,1},{17,25},{25,17},{2,10},{10... | collective-permute-start | bytes 12296 | tf_op jit(solution)/shard_map/ppermute | solution.py:385
  56.8 2.1 %collective-permute-done.14.right = f32[8,128]{1,0:T(8,128)S(1)} collective-permute-done((f32[8,128]{1,0:T(8,128)S(1)}, f32[8,128]{1,0:T(8,128)S(1)}, u32[]{:S(2)}, u32[]{:S(2)}) %collective-permute-start.14) | collective-permute-done | bytes 4128 | tf_op jit(solution)/shard_map/ppermute | solution.py:385
  58.9 2.7 %scale.1 = (bf16[1536,768]{1,0:T(8,128)(2,1)}, bf16[512,512]{1,0:T(8,128)(2,1)}, bf16[512,512]{1,0:T(8,128)(2,1)}, f32[32,1536]{1,0:T(8,128)}, f32[32,576]{1,0:T(8,128)}) custom-call(f32[8,128]{1,0:T(8,128)S(1)} %add.15.left, f32[8,128]{1,0:T(8,128)S(1)} %collective-permute-done.14.right, f32[1536,768]{1,0:T(8,128)S(1)} %get-tuple-element.111.sq, ...), custom_call_target="tpu_custom_call" | custom-call | tf_op jit(solution)/shard_map/scale/pallas_call | solution.py:583
  (21 shorter events, 3.3 us)
Async XLA Ops:
  2.5 21.6 %collective-permute-start.1 = (bf16[128,3200]{1,0:T(8,128)(2,1)S(1)}, bf16[128,3200]{1,0:T(8,128)(2,1)S(1)}, u32[]{:S(2)}, u32[]{:S(2)}) collective-permute-start(bf16[128,3200]{1,0:T(8,128)(2,1)S(1)} %load.1), channel_id=1, source_target_pairs={{0,8},{1,17},{2,10},{3,19},{4,12},{5,21},{6,14},{7,23},{8,0},{9,25... | collective-permute-start | bytes 2457608 | tf_op jit(solution)/shard_map/ppermute | solution.py:402
  5.5 18.6 %collective-permute-start = (bf16[128,3200]{1,0:T(8,128)(2,1)S(1)}, bf16[128,3200]{1,0:T(8,128)(2,1)S(1)}, u32[]{:S(2)}, u32[]{:S(2)}) collective-permute-start(bf16[128,3200]{1,0:T(8,128)(2,1)S(1)} %load.1), channel_id=1, source_target_pairs={{0,16},{1,9},{2,18},{3,11},{4,20},{5,13},{6,22},{7,15},{8,24},{9,1... | collective-permute-start | bytes 2457608 | tf_op jit(solution)/shard_map/ppermute | solution.py:402
  13.1 1.6 %collective-permute-start.2 = (bf16[64,2176]{1,0:T(8,128)(2,1)S(1)}, bf16[64,2176]{1,0:T(8,128)(2,1)S(1)}, u32[]{:S(2)}, u32[]{:S(2)}) collective-permute-start(bf16[64,2176]{1,0:T(8,128)(2,1)S(1)} %get-tuple-element.71), channel_id=1, source_target_pairs={{0,1},{1,0},{2,3},{3,2},{4,5},{5,4},{6,7},{7,6},{8,9},{9,8},{10,11... | collective-permute-start | bytes 835592 | tf_op jit(solution)/shard_map/ppermute | solution.py:385
  13.2 1.9 %collective-permute-start.3 = (bf16[64,2176]{1,0:T(8,128)(2,1)S(1)}, bf16[64,2176]{1,0:T(8,128)(2,1)S(1)}, u32[]{:S(2)}, u32[]{:S(2)}) collective-permute-start(bf16[64,2176]{1,0:T(8,128)(2,1)S(1)} %get-tuple-element.72), channel_id=1, source_target_pairs={{0,1},{1,0},{2,3},{3,2},{4,5},{5,4},{6,7},{7,6},{8,9},{9,8},{10,11... | collective-permute-start | bytes 835592 | tf_op jit(solution)/shard_map/ppermute | solution.py:385
  15.3 8.8 %collective-permute-start.4 = (bf16[64,2176]{1,0:T(8,128)(2,1)S(1)}, bf16[64,2176]{1,0:T(8,128)(2,1)S(1)}, u32[]{:S(2)}, u32[]{:S(2)}) collective-permute-start(bf16[64,2176]{1,0:T(8,128)(2,1)S(1)} %get-tuple-element.73), channel_id=1, source_target_pairs={{0,2},{1,3},{2,0},{3,1},{4,6},{5,7},{6,4},{7,5},{8,10},{9,11},{10,... | collective-permute-start | bytes 835592 | tf_op jit(solution)/shard_map/ppermute | solution.py:385
  24.0 2.9 %collective-permute-start.7 = (bf16[128,3200]{1,0:T(8,128)(2,1)S(1)}, bf16[128,3200]{1,0:T(8,128)(2,1)S(1)}, u32[]{:S(2)}, u32[]{:S(2)}) collective-permute-start(bf16[128,3200]{1,0:T(8,128)(2,1)S(1)} %collective-permute-done.1.refs_0_), channel_id=1, source_target_pairs={{0,1},{1,0},{2,3},{3,2},{4,5},{5,4},{6,7},{7,6},{8,9},{9,8},{10,11... | collective-permute-start | bytes 2457608 | tf_op jit(solution)/shard_map/ppermute | solution.py:385
  24.4 3.2 %collective-permute-start.6 = (bf16[128,3200]{1,0:T(8,128)(2,1)S(1)}, bf16[128,3200]{1,0:T(8,128)(2,1)S(1)}, u32[]{:S(2)}, u32[]{:S(2)}) collective-permute-start(bf16[128,3200]{1,0:T(8,128)(2,1)S(1)} %collective-permute-done.refs_2_), channel_id=1, source_target_pairs={{0,1},{1,0},{2,3},{3,2},{4,5},{5,4},{6,7},{7,6},{8,9},{9,8},{10,11... | collective-permute-start | bytes 2457608 | tf_op jit(solution)/shard_map/ppermute | solution.py:385
  24.6 12.7 %collective-permute-start.5 = (bf16[128,3200]{1,0:T(8,128)(2,1)S(1)}, bf16[128,3200]{1,0:T(8,128)(2,1)S(1)}, u32[]{:S(2)}, u32[]{:S(2)}) collective-permute-start(bf16[128,3200]{1,0:T(8,128)(2,1)S(1)} %collective-permute-done.refs_2_), channel_id=1, source_target_pairs={{0,8},{1,17},{2,10},{3,19},{4,12},{5,21},{6,14},{7,23},{8,0},{9,25... | collective-permute-start | bytes 2457608 | tf_op jit(solution)/shard_map/ppermute | solution.py:402
  37.3 4.4 %collective-permute-start.8 = (bf16[128,3200]{1,0:T(8,128)(2,1)S(1)}, bf16[128,3200]{1,0:T(8,128)(2,1)S(1)}, u32[]{:S(2)}, u32[]{:S(2)}) collective-permute-start(bf16[128,3200]{1,0:T(8,128)(2,1)S(1)} %collective-permute-done.5.refs_0_), channel_id=1, source_target_pairs={{0,1},{1,0},{2,3},{3,2},{4,5},{5,4},{6,7},{7,6},{8,9},{9,8},{10,11... | collective-permute-start | bytes 2457608 | tf_op jit(solution)/shard_map/ppermute | solution.py:385
  37.4 13.1 %collective-permute-start.12 = (bf16[32,2176]{1,0:T(8,128)(2,1)S(1)}, bf16[32,2176]{1,0:T(8,128)(2,1)S(1)}, u32[]{:S(2)}, u32[]{:S(2)}) collective-permute-start(bf16[32,2176]{1,0:T(8,128)(2,1)S(1)} %get-tuple-element.99), channel_id=1, source_target_pairs={{0,4},{1,5},{2,6},{3,7},{4,0},{5,1},{6,2},{7,3},{8,12},{9,13},{10,... | collective-permute-start | bytes 417800 | tf_op jit(solution)/shard_map/ppermute | solution.py:385
  40.6 1.2 %collective-permute-start.9 = (f32[8,128]{1,0:T(8,128)S(1)}, f32[8,128]{1,0:T(8,128)S(1)}, u32[]{:S(2)}, u32[]{:S(2)}) collective-permute-start(f32[8,128]{1,0:T(8,128)S(1)} %get-tuple-element.92.refs_0_), channel_id=1, source_target_pairs={{0,1},{1,0},{2,3},{3,2},{4,5},{5,4},{6,7},{7,6},{8,9},{9,8},{10,11... | collective-permute-start | bytes 12296 | tf_op jit(solution)/shard_map/ppermute | solution.py:385
  41.7 6.3 %collective-permute-start.10 = (f32[8,128]{1,0:T(8,128)S(1)}, f32[8,128]{1,0:T(8,128)S(1)}, u32[]{:S(2)}, u32[]{:S(2)}) collective-permute-start(f32[8,128]{1,0:T(8,128)S(1)} %add.12.refs_0_), channel_id=1, source_target_pairs={{0,4},{1,5},{2,6},{3,7},{4,0},{5,1},{6,2},{7,3},{8,12},{9,13},{10,... | collective-permute-start | bytes 12296 | tf_op jit(solution)/shard_map/ppermute | solution.py:385
  48.1 3.6 %collective-permute-start.11 = (f32[8,128]{1,0:T(8,128)S(1)}, f32[8,128]{1,0:T(8,128)S(1)}, u32[]{:S(2)}, u32[]{:S(2)}) collective-permute-start(f32[8,128]{1,0:T(8,128)S(1)} %add.13.refs_0_), channel_id=1, source_target_pairs={{0,2},{1,3},{2,0},{3,1},{4,6},{5,7},{6,4},{7,5},{8,10},{9,11},{10,... | collective-permute-start | bytes 12296 | tf_op jit(solution)/shard_map/ppermute | solution.py:385
  51.7 3.6 %collective-permute-start.13 = (f32[8,128]{1,0:T(8,128)S(1)}, f32[8,128]{1,0:T(8,128)S(1)}, u32[]{:S(2)}, u32[]{:S(2)}) collective-permute-start(f32[8,128]{1,0:T(8,128)S(1)} %add.14.refs_0_), channel_id=1, source_target_pairs={{0,16},{8,24},{16,0},{24,8},{1,17},{9,25},{17,1},{25,9},{2,18},{10... | collective-permute-start | bytes 12296 | tf_op jit(solution)/shard_map/ppermute | solution.py:385
  55.3 3.6 %collective-permute-start.14 = (f32[8,128]{1,0:T(8,128)S(1)}, f32[8,128]{1,0:T(8,128)S(1)}, u32[]{:S(2)}, u32[]{:S(2)}) collective-permute-start(f32[8,128]{1,0:T(8,128)S(1)} %add.15.left), channel_id=1, source_target_pairs={{0,8},{8,0},{16,24},{24,16},{1,9},{9,1},{17,25},{25,17},{2,10},{10... | collective-permute-start | bytes 12296 | tf_op jit(solution)/shard_map/ppermute | solution.py:385
